TPU v7x, 256 devices: a whole 4x4x8 slice. The times are simulated.
256 devices in a mesh: blk: 16 (over x, y_lo, core), wide: 16 (over y_hi, z).
Axes of the slice: x: 4, y: 4 (y_hi: 2, y_lo: 2; y = y_hi * 2 + y_lo), z: 8, core: 2. Of those that a mesh axis runs over, the one named last changes fastest.
Arguments:
- points: bfloat16 [65536, 32], P(('blk', 'wide')), may hold values from -6 to 6
- inv_length: float32 [32], replicated, may hold values from 0.2 to 0.7
- noise_var: float32 [], replicated, may hold values from 0.1 to 1
- solution: float32 [65536, 128], P(('blk', 'wide')), may hold values from -6 to 6
- residual: float32 [65536, 128], P(('blk', 'wide')), may hold values from -6 to 6
- direction: float32 [65536, 128], P(('blk', 'wide')), may hold values from -6 to 6
Outputs:
- new_solution: float32 [65536, 128], P(('blk', 'wide'))
- new_residual: float32 [65536, 128], P(('blk', 'wide'))
- new_direction: float32 [65536, 128], P(('blk', 'wide'))
All inputs are finite; a program needn't handle non-finite values.
Results may differ from a plain program's by a relative error of at most 0.01.
Values may be sent and summed in bfloat16 or wider, within the bound.
No kernel may reach another device: no remote copies, remote signals or barrier semaphores. Data moves between devices by JAX's collectives and lax.ppermute only.
A program may use at most 64 MiB of HBM per device.

v0:
```python
import functools
import jax
import jax.numpy as jnp
from jax import lax
from jax.sharding import Mesh
from jax.sharding import PartitionSpec as P

WIDE = ("wide_0", "wide_1")
BLK = ("blk_0", "blk_1", "blk_2")
BLK_WIDE = ("blk_0", "blk_1", "blk_2", "wide_0", "wide_1")


def shifted(x, axis, by):
    count = lax.axis_size(axis)
    return lax.ppermute(x, axis, [(i, (i + by) % count) for i in range(count)])


def cut_along(x, dim, count):
    before, after = (x.shape[:dim], x.shape[dim + 1 :])
    return jnp.moveaxis(x.reshape(*before, count, -1, *after), dim, 0)


def sent_and_summed(x, axis, dim):
    count = lax.axis_size(axis)
    blocks = lax.all_to_all(cut_along(x, dim, count), axis, 0, 0, tiled=True)
    return jnp.sum(blocks.astype(jnp.float32), axis=0)


def over_axes(x, axes):
    return functools.reduce(lax.psum, axes, x)


def squares_of(values):
    wide_values = values.astype(jnp.float32)
    return jnp.sum(wide_values * wide_values, axis=1)


def kernel_tile(rows_x, rows_sq, cols_x, cols_sq):
    inner_prod = lax.dot_general(
        rows_x, cols_x, (((1,), (1,)), ((), ())), preferred_element_type=jnp.float32
    )
    dist_sq = jnp.maximum(rows_sq[:, None] + cols_sq[None, :] - 2.0 * inner_prod, 0.0)
    radius = jnp.sqrt(5.0 * dist_sq)
    return ((1.0 + radius + radius * radius / 3.0) * jnp.exp(-radius)).astype(jnp.bfloat16)


def on_device(points, inv_length, noise_var, solution, residual, direction):
    scaled = (points.astype(jnp.float32) * inv_length).astype(jnp.bfloat16)
    low_dir = direction.astype(jnp.bfloat16)
    own_sq = squares_of(scaled)
    block_x, block_p = (
        lax.all_gather(scaled, WIDE, axis=0, tiled=True),
        lax.all_gather(low_dir, WIDE, axis=0, tiled=True),
    )
    block_sq = squares_of(block_x)
    cycle_size = lax.axis_size(BLK)
    empty_sums = jnp.zeros(direction.shape, jnp.float32)
    half_cycle = cycle_size // 2
    row_sums = jnp.dot(
        kernel_tile(block_x, block_sq, scaled, own_sq), low_dir, preferred_element_type=jnp.float32
    )

    def paired_turn(counter, carried):
        piece_x, piece_p, piece_sum, row_total = carried
        piece_x, piece_p = shifted((piece_x, piece_p), BLK, 1)
        piece_sum = shifted(piece_sum, BLK, 1)
        kernel_block = kernel_tile(block_x, block_sq, piece_x, squares_of(piece_x))
        row_total = row_total + jnp.dot(kernel_block, piece_p, preferred_element_type=jnp.float32)
        piece_sum = piece_sum + lax.dot_general(
            kernel_block, block_p, (((0,), (0,)), ((), ())), preferred_element_type=jnp.float32
        )
        return (piece_x, piece_p, piece_sum, row_total)

    result = lax.fori_loop(0, half_cycle - 1, paired_turn, (scaled, low_dir, empty_sums, row_sums))
    home_sums = shifted(result[2], BLK, 1 - half_cycle)
    far_x, far_p = shifted((scaled, low_dir), BLK, half_cycle)
    far_block = kernel_tile(block_x, block_sq, far_x, squares_of(far_x))
    row_sums = result[3] + jnp.dot(far_block, far_p, preferred_element_type=jnp.float32)
    own_image = sent_and_summed(row_sums.astype(jnp.bfloat16), WIDE, 0) + home_sums
    kernel_image = own_image + noise_var * direction
    old_norm = over_axes(jnp.sum(residual * residual, axis=0), BLK_WIDE)
    curvature = over_axes(jnp.sum(direction * kernel_image, axis=0), BLK_WIDE)
    step_length = old_norm / curvature
    new_residual = residual - step_length * kernel_image
    new_norm = over_axes(jnp.sum(new_residual * new_residual, axis=0), BLK_WIDE)
    new_solution = solution + step_length * direction
    new_direction = new_residual + new_norm / old_norm * direction
    return (new_solution, new_residual, new_direction)


def solution(mesh):
    finer = Mesh(
        mesh.devices.reshape(4, 2, 2, 2, 8), ("blk_0", "blk_1", "blk_2", "wide_0", "wide_1")
    )
    placed = (P(BLK_WIDE, None), P(), P(), P(BLK_WIDE, None), P(BLK_WIDE, None), P(BLK_WIDE, None))
    return jax.shard_map(
        on_device,
        mesh=finer,
        in_specs=placed,
        out_specs=(P(BLK_WIDE, None), P(BLK_WIDE, None), P(BLK_WIDE, None)),
        check_vma=False,
    )
```

profile of v0, /device:TPU:10, one launch (start us, length us, event | category | flops | bytes accessed | tf_op | source)
XLA Modules:
  0.0 301.9 jit_solution(7086538707987538601)
XLA Ops:
  7.2 1.5 convert_element_type.38
  8.8 2.2 collective-permute-start.4
  11.8 1.3 multiply_reduce_fusion.5
  13.1 1.4 collective-permute-start.3
  14.5 50.2 %all_gather.6 = bf16[4096,32]{1,0:T(8,128)(2,1)S(1)} all-gather(bf16[256,32]{1,0:T(8,128)(2,1)} %get-tuple-element.156), channel_id=1, replica_groups=mesh['blk_0'=4,'blk_1'=2,'blk_2'=2,'wide_0'=2,'wide_1'=8] {'wide_0','wid..., dimensions={0}, use_global_device_ids=true | all-gather | bytes 278528 | tf_op jit(solution)/shard_map/all_gather | solution.py:52
  65.4 3.8 %fusion.5 = f32[4096,128]{1,0:T(8,128)S(1)} fusion(bf16[256,128]{1,0:T(8,128)(2,1)S(1)} %copy-done.4, bf16[4096,32]{1,0:T(8,128)(2,1)S(1)} %all_gather.6, bf16[256,32]{1,0:T(8,128)(2,1)} %get-tuple-element.156, f32[256]{0:T(256)S(1)} %get-tuple-element.103, f32[4096]{0:T(1024)S(1)} %multiply_reduce_fusion.1), kind=kOutput, calls=%fused_computation.18 | convolution fusion | flops 348127232 | bytes 2458624 | tf_op jit(solution)/shard_map/dot_general | solution.py:59
  69.9 22.2 %all-gather.2.cloned.1.call-done = bf16[4096,128]{1,0:T(8,128)(2,1)} async-done(((bf16[256,128]{1,0:T(8,128)(2,1)}), bf16[4096,128]{1,0:T(8,128)(2,1)}) %all-gather.2.cloned.1.call-update) | async-done | bytes 1048592 | tf_op jit(solution)/shard_map/all_gather | solution.py:53
  92.1 79.3 %while.17 = (s32[]{:T(128)}, bf16[256,32]{1,0:T(8,128)(2,1)}, bf16[256,128]{1,0:T(8,128)(2,1)S(1)}, f32[256,128]{1,0:T(8,128)S(1)}, f32[4096,128]{1,0:T(8,128)S(...) while((s32[]{:T(128)}, bf16[256,32]{1,0:T(8,128)(2,1)}, ...), condition=%wide.region_10.0_spmd.clone, body=%wide.region_8.10_spmd.clone.sunk | while | flops 617176832 | bytes 17647876 | solution.py:74
  92.1 2.5 collective-permute-start.2
  94.7 1.3 collective-permute-done
  96.1 3.1 %multiply_convert_fusion.6 = bf16[4096,256]{1,0:T(8,128)(2,1)S(1)} fusion(bf16[4096,32]{1,0:T(8,128)(2,1)S(1)} %get-tuple-element.181, bf16[256,32]{1,0:T(8,128)(2,1)S(1)} %collective-permute-done, f32[256]{0:T(256)S(1)} %multiply_reduce_fusion.8, f32[4096]{0:T(1024)S(1)} %get-tuple-element.180), kind=kOutput, calls=%fused_computation.2.clone.1 | convolution fusion | flops 79691776 | bytes 2393088 | tf_op jit(solution)/shard_map/while/body/eval_jaxpr/dot_general | solution.py:39
  101.1 1.7 convolution_add_fusion.5
  103.0 3.2 %collective-permute-start.2 = (f32[256,128]{1,0:T(8,128)S(1)}, f32[256,128]{1,0:T(8,128)}, u32[]{:S(2)}, u32[]{:S(2)}) collective-permute-start(f32[256,128]{1,0:T(8,128)S(1)} %broadcast_select_fusion.2), channel_id=1, source_target_pairs={{0,16},{16,32},{32,48},{48,64},{64,80},{80,96},{96,112},{112,128},... | collective-permute-start | bytes 393224 | tf_op jit(solution)/shard_map/while/body/eval_jaxpr/ppermute | solution.py:15
  106.8 3.1 %multiply_convert_fusion.6 = bf16[4096,256]{1,0:T(8,128)(2,1)S(1)} fusion(bf16[4096,32]{1,0:T(8,128)(2,1)S(1)} %get-tuple-element.181, bf16[256,32]{1,0:T(8,128)(2,1)S(1)} %collective-permute-done, f32[256]{0:T(256)S(1)} %multiply_reduce_fusion.8, f32[4096]{0:T(1024)S(1)} %get-tuple-element.180), kind=kOutput, calls=%fused_computation.2.clone.1 | convolution fusion | flops 79691776 | bytes 2393088 | tf_op jit(solution)/shard_map/while/body/eval_jaxpr/dot_general | solution.py:39
  111.8 1.7 convolution_add_fusion.5
  114.7 3.2 %collective-permute-start.2 = (f32[256,128]{1,0:T(8,128)S(1)}, f32[256,128]{1,0:T(8,128)}, u32[]{:S(2)}, u32[]{:S(2)}) collective-permute-start(f32[256,128]{1,0:T(8,128)S(1)} %broadcast_select_fusion.2), channel_id=1, source_target_pairs={{0,16},{16,32},{32,48},{48,64},{64,80},{80,96},{96,112},{112,128},... | collective-permute-start | bytes 393224 | tf_op jit(solution)/shard_map/while/body/eval_jaxpr/ppermute | solution.py:15
  118.1 3.1 %multiply_convert_fusion.6 = bf16[4096,256]{1,0:T(8,128)(2,1)S(1)} fusion(bf16[4096,32]{1,0:T(8,128)(2,1)S(1)} %get-tuple-element.181, bf16[256,32]{1,0:T(8,128)(2,1)S(1)} %collective-permute-done, f32[256]{0:T(256)S(1)} %multiply_reduce_fusion.8, f32[4096]{0:T(1024)S(1)} %get-tuple-element.180), kind=kOutput, calls=%fused_computation.2.clone.1 | convolution fusion | flops 79691776 | bytes 2393088 | tf_op jit(solution)/shard_map/while/body/eval_jaxpr/dot_general | solution.py:39
  123.1 1.7 convolution_add_fusion.5
  124.8 1.5 collective-permute-start
  126.3 3.2 %collective-permute-start.2 = (f32[256,128]{1,0:T(8,128)S(1)}, f32[256,128]{1,0:T(8,128)}, u32[]{:S(2)}, u32[]{:S(2)}) collective-permute-start(f32[256,128]{1,0:T(8,128)S(1)} %broadcast_select_fusion.2), channel_id=1, source_target_pairs={{0,16},{16,32},{32,48},{48,64},{64,80},{80,96},{96,112},{112,128},... | collective-permute-start | bytes 393224 | tf_op jit(solution)/shard_map/while/body/eval_jaxpr/ppermute | solution.py:15
  129.8 3.1 %multiply_convert_fusion.6 = bf16[4096,256]{1,0:T(8,128)(2,1)S(1)} fusion(bf16[4096,32]{1,0:T(8,128)(2,1)S(1)} %get-tuple-element.181, bf16[256,32]{1,0:T(8,128)(2,1)S(1)} %collective-permute-done, f32[256]{0:T(256)S(1)} %multiply_reduce_fusion.8, f32[4096]{0:T(1024)S(1)} %get-tuple-element.180), kind=kOutput, calls=%fused_computation.2.clone.1 | convolution fusion | flops 79691776 | bytes 2393088 | tf_op jit(solution)/shard_map/while/body/eval_jaxpr/dot_general | solution.py:39
  134.7 1.7 convolution_add_fusion.5
  136.4 1.5 collective-permute-start
  138.0 3.2 %collective-permute-start.2 = (f32[256,128]{1,0:T(8,128)S(1)}, f32[256,128]{1,0:T(8,128)}, u32[]{:S(2)}, u32[]{:S(2)}) collective-permute-start(f32[256,128]{1,0:T(8,128)S(1)} %broadcast_select_fusion.2), channel_id=1, source_target_pairs={{0,16},{16,32},{32,48},{48,64},{64,80},{80,96},{96,112},{112,128},... | collective-permute-start | bytes 393224 | tf_op jit(solution)/shard_map/while/body/eval_jaxpr/ppermute | solution.py:15
  141.4 3.1 %multiply_convert_fusion.6 = bf16[4096,256]{1,0:T(8,128)(2,1)S(1)} fusion(bf16[4096,32]{1,0:T(8,128)(2,1)S(1)} %get-tuple-element.181, bf16[256,32]{1,0:T(8,128)(2,1)S(1)} %collective-permute-done, f32[256]{0:T(256)S(1)} %multiply_reduce_fusion.8, f32[4096]{0:T(1024)S(1)} %get-tuple-element.180), kind=kOutput, calls=%fused_computation.2.clone.1 | convolution fusion | flops 79691776 | bytes 2393088 | tf_op jit(solution)/shard_map/while/body/eval_jaxpr/dot_general | solution.py:39
  146.4 1.7 convolution_add_fusion.5
  148.1 1.5 collective-permute-start
  149.6 3.2 %collective-permute-start.2 = (f32[256,128]{1,0:T(8,128)S(1)}, f32[256,128]{1,0:T(8,128)}, u32[]{:S(2)}, u32[]{:S(2)}) collective-permute-start(f32[256,128]{1,0:T(8,128)S(1)} %broadcast_select_fusion.2), channel_id=1, source_target_pairs={{0,16},{16,32},{32,48},{48,64},{64,80},{80,96},{96,112},{112,128},... | collective-permute-start | bytes 393224 | tf_op jit(solution)/shard_map/while/body/eval_jaxpr/ppermute | solution.py:15
  153.1 3.1 %multiply_convert_fusion.6 = bf16[4096,256]{1,0:T(8,128)(2,1)S(1)} fusion(bf16[4096,32]{1,0:T(8,128)(2,1)S(1)} %get-tuple-element.181, bf16[256,32]{1,0:T(8,128)(2,1)S(1)} %collective-permute-done, f32[256]{0:T(256)S(1)} %multiply_reduce_fusion.8, f32[4096]{0:T(1024)S(1)} %get-tuple-element.180), kind=kOutput, calls=%fused_computation.2.clone.1 | convolution fusion | flops 79691776 | bytes 2393088 | tf_op jit(solution)/shard_map/while/body/eval_jaxpr/dot_general | solution.py:39
  158.0 1.7 convolution_add_fusion.5
  159.7 1.5 collective-permute-start
  161.3 3.2 %collective-permute-start.2 = (f32[256,128]{1,0:T(8,128)S(1)}, f32[256,128]{1,0:T(8,128)}, u32[]{:S(2)}, u32[]{:S(2)}) collective-permute-start(f32[256,128]{1,0:T(8,128)S(1)} %broadcast_select_fusion.2), channel_id=1, source_target_pairs={{0,16},{16,32},{32,48},{48,64},{64,80},{80,96},{96,112},{112,128},... | collective-permute-start | bytes 393224 | tf_op jit(solution)/shard_map/while/body/eval_jaxpr/ppermute | solution.py:15
  164.7 3.1 %multiply_convert_fusion.6 = bf16[4096,256]{1,0:T(8,128)(2,1)S(1)} fusion(bf16[4096,32]{1,0:T(8,128)(2,1)S(1)} %get-tuple-element.181, bf16[256,32]{1,0:T(8,128)(2,1)S(1)} %collective-permute-done, f32[256]{0:T(256)S(1)} %multiply_reduce_fusion.8, f32[4096]{0:T(1024)S(1)} %get-tuple-element.180), kind=kOutput, calls=%fused_computation.2.clone.1 | convolution fusion | flops 79691776 | bytes 2393088 | tf_op jit(solution)/shard_map/while/body/eval_jaxpr/dot_general | solution.py:39
  169.7 1.7 convolution_add_fusion.5
  171.3 5.0 %fusion.4 = bf16[4096,128]{1,0:T(8,128)(2,1)} fusion(f32[4096,128]{1,0:T(8,128)S(1)} %get-tuple-element.46, bf16[256,128]{1,0:T(8,128)(2,1)} %copy-done.7, f32[256]{0:T(256)} %multiply_reduce_fusion.4, bf16[4096,32]{1,0:T(8,128)(2,1)S(1)} %get-tuple-element.189, bf16[256,32]{1,0:T(8,128)(2,1)} %copy-done.6, f32[4096]{0:T(1024)S(1)} %get-tuple-element.201), kind=kOutput, calls=%fused_computation.13 | convolution fusion | flops 349175808 | bytes 3507200 | tf_op jit(solution)/shard_map/dot_general | solution.py:78
  176.3 4.4 %all-to-all-start = ((bf16[16,256,128]{2,1,0:T(8,128)(2,1)}), bf16[16,256,128]{2,1,0:T(8,128)(2,1)S(1)}, u32[]{:S(2)}, u32[]{:S(2)}) async-start(bf16[16,256,128]{2,1,0:T(8,128)(2,1)} %bitcast.25), calls=%async_computation | async-start | bytes 2097152 | tf_op jit(solution)/shard_map/all_to_all | solution.py:25
  181.4 9.2 %collective-permute-start.5 = (f32[256,128]{1,0:T(8,128)S(1)}, f32[256,128]{1,0:T(8,128)S(1)}, u32[]{:S(2)}, u32[]{:S(2)}) collective-permute-start(f32[256,128]{1,0:T(8,128)S(1)} %get-tuple-element.47), channel_id=1, source_target_pairs={{0,144},{16,160},{32,176},{48,192},{64,208},{80,224},{96,240},{112... | collective-permute-start | bytes 393224 | tf_op jit(solution)/shard_map/ppermute | solution.py:15
  190.6 20.1 %all-to-all-done = bf16[16,256,128]{2,1,0:T(8,128)(2,1)S(1)} async-done(((bf16[16,256,128]{2,1,0:T(8,128)(2,1)}), bf16[16,256,128]{2,1,0:T(8,128)(2,1)S(1)}, u32[]{:S(2)}, u32[]{:S(2)}) %all-to-all-start) | async-done | bytes 1048608 | tf_op jit(solution)/shard_map/all_to_all | solution.py:25
  210.9 13.9 %all-reduce.1 = (f32[128]{0:T(128)S(1)}, f32[128]{0:T(128)S(1)}) all-reduce(f32[128]{0:T(128)S(1)} %multiply_reduce_fusion.6, f32[128]{0:T(128)S(1)} %multiply_reduce_fusion.3), channel_id=1, replica_groups=mesh['blk_0'=4,'blk_1'=2,'blk_2'=2,'wide_0'=2,'wide_1'=8] {'blk_0'}, use_global_device_ids=true, to_apply=%region_1.0 | all-reduce | flops 256 | bytes 2048 | tf_op jit(solution)/shard_map/psum | solution.py:30
  224.8 4.9 %all-reduce.4 = (f32[128]{0:T(128)S(1)}, f32[128]{0:T(128)S(1)}) all-reduce(f32[128]{0:T(128)S(1)} %get-tuple-element.93, f32[128]{0:T(128)S(1)} %get-tuple-element.94), channel_id=1, replica_groups=mesh['blk_0'=4,'blk_1'=2,'blk_2'=2,'wide_0'=2,'wide_1'=8] {'blk_1'}, use_global_device_ids=true, to_apply=%region_2.3 | all-reduce | flops 256 | bytes 2048 | tf_op jit(solution)/shard_map/psum | solution.py:30
  229.8 2.4 all-reduce.3
  232.2 6.4 %all-reduce.2 = (f32[128]{0:T(128)S(1)}, f32[128]{0:T(128)S(1)}) all-reduce(f32[128]{0:T(128)S(1)} %get-tuple-element.97, f32[128]{0:T(128)S(1)} %get-tuple-element.98), channel_id=1, replica_groups=mesh['blk_0'=4,'blk_1'=2,'blk_2'=2,'wide_0'=2,'wide_1'=8] {'wide_0'}, use_global_device_ids=true, to_apply=%region_4.0 | all-reduce | flops 256 | bytes 2048 | tf_op jit(solution)/shard_map/psum | solution.py:30
  238.6 15.1 %all-reduce = (f32[128]{0:T(128)S(1)}, f32[128]{0:T(128)S(1)}) all-reduce(f32[128]{0:T(128)S(1)} %get-tuple-element.95, f32[128]{0:T(128)S(1)} %get-tuple-element.96), channel_id=1, replica_groups=mesh['blk_0'=4,'blk_1'=2,'blk_2'=2,'wide_0'=2,'wide_1'=8] {'wide_1'}, use_global_device_ids=true, to_apply=%region_5.0 | all-reduce | flops 256 | bytes 2048 | tf_op jit(solution)/shard_map/psum | solution.py:30
  254.4 10.9 %psum.115 = f32[128]{0:T(128)S(1)} all-reduce(f32[128]{0:T(128)S(1)} %get-tuple-element.101), channel_id=1, replica_groups=mesh['blk_0'=4,'blk_1'=2,'blk_2'=2,'wide_0'=2,'wide_1'=8] {'blk_0'}, use_global_device_ids=true, to_apply=%region_20.0 | all-reduce | flops 128 | bytes 1024 | tf_op jit(solution)/shard_map/psum | solution.py:30
  265.4 4.9 %psum.116 = f32[128]{0:T(128)S(1)} all-reduce(f32[128]{0:T(128)S(1)} %psum.115), channel_id=1, replica_groups=mesh['blk_0'=4,'blk_1'=2,'blk_2'=2,'wide_0'=2,'wide_1'=8] {'blk_1'}, use_global_device_ids=true, to_apply=%region_21.0 | all-reduce | flops 128 | bytes 1024 | tf_op jit(solution)/shard_map/psum | solution.py:30
  270.3 2.4 psum.117
  272.7 6.4 %psum.118 = f32[128]{0:T(128)S(1)} all-reduce(f32[128]{0:T(128)S(1)} %psum.117), channel_id=1, replica_groups=mesh['blk_0'=4,'blk_1'=2,'blk_2'=2,'wide_0'=2,'wide_1'=8] {'wide_0'}, use_global_device_ids=true, to_apply=%region_23.0 | all-reduce | flops 128 | bytes 1024 | tf_op jit(solution)/shard_map/psum | solution.py:30
  279.2 15.2 %psum.119 = f32[128]{0:T(128)S(1)} all-reduce(f32[128]{0:T(128)S(1)} %psum.118), channel_id=1, replica_groups=mesh['blk_0'=4,'blk_1'=2,'blk_2'=2,'wide_0'=2,'wide_1'=8] {'wide_1'}, use_global_device_ids=true, to_apply=%region_24.0 | all-reduce | flops 128 | bytes 1024 | tf_op jit(solution)/shard_map/psum | solution.py:30
  (109 shorter events, 20.1 us)
Async XLA Ops:
  7.2 84.9 %all-gather.2.cloned.1.call-start = ((), (), s32[]{:S(2)}) async-start(), calls=%async_computation.1 | async-start | bytes 1114112 | tf_op jit(solution)/shard_map/all_gather | solution.py:53
  8.8 56.6 %copy-start.4 = (bf16[256,128]{1,0:T(8,128)(2,1)S(1)}, bf16[256,128]{1,0:T(8,128)(2,1)}, u32[]{:S(2)}) copy-start(bf16[256,128]{1,0:T(8,128)(2,1)} %convert_element_type.38) | copy-start | bytes 196612
  8.8 61.1 %collective-permute-start.4 = (bf16[256,128]{1,0:T(8,128)(2,1)}, bf16[256,128]{1,0:T(8,128)(2,1)S(1)}, u32[]{:S(2)}, u32[]{:S(2)}) collective-permute-start(bf16[256,128]{1,0:T(8,128)(2,1)} %convert_element_type.38), channel_id=1, source_target_pairs={{0,128},{16,144},{32,160},{48,176},{64,192},{80,208},{96,224},{112... | collective-permute-start | bytes 196616 | tf_op jit(solution)/shard_map/ppermute | solution.py:15
  13.1 56.0 %collective-permute-start.3 = (bf16[256,32]{1,0:T(8,128)(2,1)}, bf16[256,32]{1,0:T(8,128)(2,1)S(1)}, u32[]{:S(2)}, u32[]{:S(2)}) collective-permute-start(bf16[256,32]{1,0:T(8,128)(2,1)} %get-tuple-element.156), channel_id=1, source_target_pairs={{0,128},{16,144},{32,160},{48,176},{64,192},{80,208},{96,224},{112... | collective-permute-start | bytes 49160 | tf_op jit(solution)/shard_map/ppermute | solution.py:15
  69.2 22.9 %copy-start.6 = (bf16[256,32]{1,0:T(8,128)(2,1)}, bf16[256,32]{1,0:T(8,128)(2,1)S(1)}, u32[]{:S(2)}) copy-start(bf16[256,32]{1,0:T(8,128)(2,1)S(1)} %collective-permute-done.3) | copy-start | bytes 49156
  69.9 22.2 %copy-start.7 = (bf16[256,128]{1,0:T(8,128)(2,1)}, bf16[256,128]{1,0:T(8,128)(2,1)S(1)}, u32[]{:S(2)}) copy-start(bf16[256,128]{1,0:T(8,128)(2,1)S(1)} %collective-permute-done.4) | copy-start | bytes 196612
  92.1 3.9 %collective-permute-start = (bf16[256,32]{1,0:T(8,128)(2,1)}, bf16[256,32]{1,0:T(8,128)(2,1)S(1)}, u32[]{:S(2)}, u32[]{:S(2)}) collective-permute-start(bf16[256,32]{1,0:T(8,128)(2,1)} %get-tuple-element.166), channel_id=1, source_target_pairs={{0,16},{16,32},{32,48},{48,64},{64,80},{80,96},{96,112},{112,128},... | collective-permute-start | bytes 49160 | tf_op jit(solution)/shard_map/while/body/eval_jaxpr/ppermute | solution.py:15
  92.1 8.5 %collective-permute-start.2 = (f32[256,128]{1,0:T(8,128)S(1)}, f32[256,128]{1,0:T(8,128)}, u32[]{:S(2)}, u32[]{:S(2)}) collective-permute-start(f32[256,128]{1,0:T(8,128)S(1)} %broadcast_select_fusion.2), channel_id=1, source_target_pairs={{0,16},{16,32},{32,48},{48,64},{64,80},{80,96},{96,112},{112,128},... | collective-permute-start | bytes 393224 | tf_op jit(solution)/shard_map/while/body/eval_jaxpr/ppermute | solution.py:15
  94.6 5.2 %collective-permute-start.1 = (bf16[256,128]{1,0:T(8,128)(2,1)S(1)}, bf16[256,128]{1,0:T(8,128)(2,1)S(1)}, u32[]{:S(2)}, u32[]{:S(2)}) collective-permute-start(bf16[256,128]{1,0:T(8,128)(2,1)S(1)} %get-tuple-element.167), channel_id=1, source_target_pairs={{0,16},{16,32},{32,48},{48,64},{64,80},{80,96},{96,112},{112,128},... | collective-permute-start | bytes 196616 | tf_op jit(solution)/shard_map/while/body/eval_jaxpr/ppermute | solution.py:15
  99.8 1.2 copy-start
  102.7 4.0 %collective-permute-start = (bf16[256,32]{1,0:T(8,128)(2,1)}, bf16[256,32]{1,0:T(8,128)(2,1)S(1)}, u32[]{:S(2)}, u32[]{:S(2)}) collective-permute-start(bf16[256,32]{1,0:T(8,128)(2,1)} %get-tuple-element.166), channel_id=1, source_target_pairs={{0,16},{16,32},{32,48},{48,64},{64,80},{80,96},{96,112},{112,128},... | collective-permute-start | bytes 49160 | tf_op jit(solution)/shard_map/while/body/eval_jaxpr/ppermute | solution.py:15
  103.0 8.3 %collective-permute-start.2 = (f32[256,128]{1,0:T(8,128)S(1)}, f32[256,128]{1,0:T(8,128)}, u32[]{:S(2)}, u32[]{:S(2)}) collective-permute-start(f32[256,128]{1,0:T(8,128)S(1)} %broadcast_select_fusion.2), channel_id=1, source_target_pairs={{0,16},{16,32},{32,48},{48,64},{64,80},{80,96},{96,112},{112,128},... | collective-permute-start | bytes 393224 | tf_op jit(solution)/shard_map/while/body/eval_jaxpr/ppermute | solution.py:15
  106.3 4.3 %collective-permute-start.1 = (bf16[256,128]{1,0:T(8,128)(2,1)S(1)}, bf16[256,128]{1,0:T(8,128)(2,1)S(1)}, u32[]{:S(2)}, u32[]{:S(2)}) collective-permute-start(bf16[256,128]{1,0:T(8,128)(2,1)S(1)} %get-tuple-element.167), channel_id=1, source_target_pairs={{0,16},{16,32},{32,48},{48,64},{64,80},{80,96},{96,112},{112,128},... | collective-permute-start | bytes 196616 | tf_op jit(solution)/shard_map/while/body/eval_jaxpr/ppermute | solution.py:15
  110.6 1.2 copy-start
  113.5 4.5 %collective-permute-start = (bf16[256,32]{1,0:T(8,128)(2,1)}, bf16[256,32]{1,0:T(8,128)(2,1)S(1)}, u32[]{:S(2)}, u32[]{:S(2)}) collective-permute-start(bf16[256,32]{1,0:T(8,128)(2,1)} %get-tuple-element.166), channel_id=1, source_target_pairs={{0,16},{16,32},{32,48},{48,64},{64,80},{80,96},{96,112},{112,128},... | collective-permute-start | bytes 49160 | tf_op jit(solution)/shard_map/while/body/eval_jaxpr/ppermute | solution.py:15
  114.7 8.0 %collective-permute-start.2 = (f32[256,128]{1,0:T(8,128)S(1)}, f32[256,128]{1,0:T(8,128)}, u32[]{:S(2)}, u32[]{:S(2)}) collective-permute-start(f32[256,128]{1,0:T(8,128)S(1)} %broadcast_select_fusion.2), channel_id=1, source_target_pairs={{0,16},{16,32},{32,48},{48,64},{64,80},{80,96},{96,112},{112,128},... | collective-permute-start | bytes 393224 | tf_op jit(solution)/shard_map/while/body/eval_jaxpr/ppermute | solution.py:15
  117.9 3.9 %collective-permute-start.1 = (bf16[256,128]{1,0:T(8,128)(2,1)S(1)}, bf16[256,128]{1,0:T(8,128)(2,1)S(1)}, u32[]{:S(2)}, u32[]{:S(2)}) collective-permute-start(bf16[256,128]{1,0:T(8,128)(2,1)S(1)} %get-tuple-element.167), channel_id=1, source_target_pairs={{0,16},{16,32},{32,48},{48,64},{64,80},{80,96},{96,112},{112,128},... | collective-permute-start | bytes 196616 | tf_op jit(solution)/shard_map/while/body/eval_jaxpr/ppermute | solution.py:15
  121.9 1.2 copy-start
  124.8 4.9 %collective-permute-start = (bf16[256,32]{1,0:T(8,128)(2,1)}, bf16[256,32]{1,0:T(8,128)(2,1)S(1)}, u32[]{:S(2)}, u32[]{:S(2)}) collective-permute-start(bf16[256,32]{1,0:T(8,128)(2,1)} %get-tuple-element.166), channel_id=1, source_target_pairs={{0,16},{16,32},{32,48},{48,64},{64,80},{80,96},{96,112},{112,128},... | collective-permute-start | bytes 49160 | tf_op jit(solution)/shard_map/while/body/eval_jaxpr/ppermute | solution.py:15
  126.3 8.0 %collective-permute-start.2 = (f32[256,128]{1,0:T(8,128)S(1)}, f32[256,128]{1,0:T(8,128)}, u32[]{:S(2)}, u32[]{:S(2)}) collective-permute-start(f32[256,128]{1,0:T(8,128)S(1)} %broadcast_select_fusion.2), channel_id=1, source_target_pairs={{0,16},{16,32},{32,48},{48,64},{64,80},{80,96},{96,112},{112,128},... | collective-permute-start | bytes 393224 | tf_op jit(solution)/shard_map/while/body/eval_jaxpr/ppermute | solution.py:15
  129.6 3.9 %collective-permute-start.1 = (bf16[256,128]{1,0:T(8,128)(2,1)S(1)}, bf16[256,128]{1,0:T(8,128)(2,1)S(1)}, u32[]{:S(2)}, u32[]{:S(2)}) collective-permute-start(bf16[256,128]{1,0:T(8,128)(2,1)S(1)} %get-tuple-element.167), channel_id=1, source_target_pairs={{0,16},{16,32},{32,48},{48,64},{64,80},{80,96},{96,112},{112,128},... | collective-permute-start | bytes 196616 | tf_op jit(solution)/shard_map/while/body/eval_jaxpr/ppermute | solution.py:15
  133.5 1.2 copy-start
  136.4 4.9 %collective-permute-start = (bf16[256,32]{1,0:T(8,128)(2,1)}, bf16[256,32]{1,0:T(8,128)(2,1)S(1)}, u32[]{:S(2)}, u32[]{:S(2)}) collective-permute-start(bf16[256,32]{1,0:T(8,128)(2,1)} %get-tuple-element.166), channel_id=1, source_target_pairs={{0,16},{16,32},{32,48},{48,64},{64,80},{80,96},{96,112},{112,128},... | collective-permute-start | bytes 49160 | tf_op jit(solution)/shard_map/while/body/eval_jaxpr/ppermute | solution.py:15
  138.0 8.0 %collective-permute-start.2 = (f32[256,128]{1,0:T(8,128)S(1)}, f32[256,128]{1,0:T(8,128)}, u32[]{:S(2)}, u32[]{:S(2)}) collective-permute-start(f32[256,128]{1,0:T(8,128)S(1)} %broadcast_select_fusion.2), channel_id=1, source_target_pairs={{0,16},{16,32},{32,48},{48,64},{64,80},{80,96},{96,112},{112,128},... | collective-permute-start | bytes 393224 | tf_op jit(solution)/shard_map/while/body/eval_jaxpr/ppermute | solution.py:15
  141.2 3.9 %collective-permute-start.1 = (bf16[256,128]{1,0:T(8,128)(2,1)S(1)}, bf16[256,128]{1,0:T(8,128)(2,1)S(1)}, u32[]{:S(2)}, u32[]{:S(2)}) collective-permute-start(bf16[256,128]{1,0:T(8,128)(2,1)S(1)} %get-tuple-element.167), channel_id=1, source_target_pairs={{0,16},{16,32},{32,48},{48,64},{64,80},{80,96},{96,112},{112,128},... | collective-permute-start | bytes 196616 | tf_op jit(solution)/shard_map/while/body/eval_jaxpr/ppermute | solution.py:15
  145.1 1.2 copy-start
  148.1 4.9 %collective-permute-start = (bf16[256,32]{1,0:T(8,128)(2,1)}, bf16[256,32]{1,0:T(8,128)(2,1)S(1)}, u32[]{:S(2)}, u32[]{:S(2)}) collective-permute-start(bf16[256,32]{1,0:T(8,128)(2,1)} %get-tuple-element.166), channel_id=1, source_target_pairs={{0,16},{16,32},{32,48},{48,64},{64,80},{80,96},{96,112},{112,128},... | collective-permute-start | bytes 49160 | tf_op jit(solution)/shard_map/while/body/eval_jaxpr/ppermute | solution.py:15
  149.6 8.0 %collective-permute-start.2 = (f32[256,128]{1,0:T(8,128)S(1)}, f32[256,128]{1,0:T(8,128)}, u32[]{:S(2)}, u32[]{:S(2)}) collective-permute-start(f32[256,128]{1,0:T(8,128)S(1)} %broadcast_select_fusion.2), channel_id=1, source_target_pairs={{0,16},{16,32},{32,48},{48,64},{64,80},{80,96},{96,112},{112,128},... | collective-permute-start | bytes 393224 | tf_op jit(solution)/shard_map/while/body/eval_jaxpr/ppermute | solution.py:15
  152.8 3.9 %collective-permute-start.1 = (bf16[256,128]{1,0:T(8,128)(2,1)S(1)}, bf16[256,128]{1,0:T(8,128)(2,1)S(1)}, u32[]{:S(2)}, u32[]{:S(2)}) collective-permute-start(bf16[256,128]{1,0:T(8,128)(2,1)S(1)} %get-tuple-element.167), channel_id=1, source_target_pairs={{0,16},{16,32},{32,48},{48,64},{64,80},{80,96},{96,112},{112,128},... | collective-permute-start | bytes 196616 | tf_op jit(solution)/shard_map/while/body/eval_jaxpr/ppermute | solution.py:15
  156.8 1.2 copy-start
  159.7 4.9 %collective-permute-start = (bf16[256,32]{1,0:T(8,128)(2,1)}, bf16[256,32]{1,0:T(8,128)(2,1)S(1)}, u32[]{:S(2)}, u32[]{:S(2)}) collective-permute-start(bf16[256,32]{1,0:T(8,128)(2,1)} %get-tuple-element.166), channel_id=1, source_target_pairs={{0,16},{16,32},{32,48},{48,64},{64,80},{80,96},{96,112},{112,128},... | collective-permute-start | bytes 49160 | tf_op jit(solution)/shard_map/while/body/eval_jaxpr/ppermute | solution.py:15
  161.3 8.0 %collective-permute-start.2 = (f32[256,128]{1,0:T(8,128)S(1)}, f32[256,128]{1,0:T(8,128)}, u32[]{:S(2)}, u32[]{:S(2)}) collective-permute-start(f32[256,128]{1,0:T(8,128)S(1)} %broadcast_select_fusion.2), channel_id=1, source_target_pairs={{0,16},{16,32},{32,48},{48,64},{64,80},{80,96},{96,112},{112,128},... | collective-permute-start | bytes 393224 | tf_op jit(solution)/shard_map/while/body/eval_jaxpr/ppermute | solution.py:15
  164.5 3.9 %collective-permute-start.1 = (bf16[256,128]{1,0:T(8,128)(2,1)S(1)}, bf16[256,128]{1,0:T(8,128)(2,1)S(1)}, u32[]{:S(2)}, u32[]{:S(2)}) collective-permute-start(bf16[256,128]{1,0:T(8,128)(2,1)S(1)} %get-tuple-element.167), channel_id=1, source_target_pairs={{0,16},{16,32},{32,48},{48,64},{64,80},{80,96},{96,112},{112,128},... | collective-permute-start | bytes 196616 | tf_op jit(solution)/shard_map/while/body/eval_jaxpr/ppermute | solution.py:15
  168.4 1.2 copy-start
  176.3 5.0 %copy-start.2 = (f32[256,128]{1,0:T(8,128)S(1)}, f32[256,128]{1,0:T(8,128)}, u32[]{:S(2)}) copy-start(f32[256,128]{1,0:T(8,128)} %param.12) | copy-start | bytes 393220
  176.3 34.5 %copy-start.1 = (f32[256,128]{1,0:T(8,128)S(1)}, f32[256,128]{1,0:T(8,128)}, u32[]{:S(2)}) copy-start(f32[256,128]{1,0:T(8,128)} %param.13) | copy-start | bytes 393220
  176.3 77.4 %copy-start.5 = (f32[256,128]{1,0:T(8,128)S(1)}, f32[256,128]{1,0:T(8,128)}, u32[]{:S(2)}) copy-start(f32[256,128]{1,0:T(8,128)} %param.11) | copy-start | bytes 393220
  176.3 34.4 %all-to-all-start = ((bf16[16,256,128]{2,1,0:T(8,128)(2,1)}), bf16[16,256,128]{2,1,0:T(8,128)(2,1)S(1)}, u32[]{:S(2)}, u32[]{:S(2)}) async-start(bf16[16,256,128]{2,1,0:T(8,128)(2,1)} %bitcast.25), calls=%async_computation | async-start | bytes 2097152 | tf_op jit(solution)/shard_map/all_to_all | solution.py:25
  181.4 29.4 %collective-permute-start.5 = (f32[256,128]{1,0:T(8,128)S(1)}, f32[256,128]{1,0:T(8,128)S(1)}, u32[]{:S(2)}, u32[]{:S(2)}) collective-permute-start(f32[256,128]{1,0:T(8,128)S(1)} %get-tuple-element.47), channel_id=1, source_target_pairs={{0,144},{16,160},{32,176},{48,192},{64,208},{80,224},{96,240},{112... | collective-permute-start | bytes 393224 | tf_op jit(solution)/shard_map/ppermute | solution.py:15
  254.4 40.6 %copy-start.3 = (f32[256,128]{1,0:T(8,128)}, f32[256,128]{1,0:T(8,128)S(1)}, u32[]{:S(2)}) copy-start(f32[256,128]{1,0:T(8,128)S(1)} %get-tuple-element.102) | copy-start | bytes 393220
Sparse Core Ops, SparseCore 0:
  11.2 80.8 all-gather.1
where the time goes:
time: 303 us; the launch traced here: 302 us
  blocking collectives  133 us (44%)
  matrix products  47.5 us (16%)
  starting transfers between devices  47.4 us (16%)
  waiting for transfers between devices  43.9 us (14%)
  between operations  14.8 us (5%)
  local copies, waits for them, and re-layouts  8.25 us (3%)
  other arithmetic  6.69 us (2%)
    psum x10, blocking collectives, over_axes(): return functools.reduce(lax.psum, axes, x)  82.7 us
    all_gather x1, blocking collectives, on_device(): lax.all_gather(scaled, WIDE, axis=0, tiled=True)  50.2 us
    ppermute x24, starting transfers between devices, shifted(): return lax.ppermute(x, axis, [(i, (i + by) % count) for i in range(count)])  43 us
    all_gather x1, waiting for transfers between devices, on_device(): lax.all_gather(low_dir, WIDE, axis=0, tiled=True)  22.2 us
    dot_general x7, matrix products, kernel_tile(): lax.dot_general(rows_x, cols_x, (((1,), (1,)), ((), ())), preferred_eleme...  21.6 us
    all_to_all x1, waiting for transfers between devices, sent_and_summed(): blocks = lax.all_to_all(cut_along(x, dim, count), axis, 0, 0, tiled=True)  20.1 us
    dot_general x7, matrix products, paired_turn(): lax.dot_general(kernel_block, block_p, (((0,), (0,)), ((), ())), preferre...  11.7 us
    while x28, local copies, waits for them, and re-layouts  7.39 us
  transfers between devices with their start and end apart: 26, of which 4 were waited for; matrix products, arithmetic and copies ran while one was open for 13% of the time, Pallas kernels for 0%

commit v1 on v0

--- a/solution.py
+++ b/solution.py
@@ -50,7 +50,9 @@
     own_sq = squares_of(scaled)
     block_x, block_p = (
         lax.all_gather(scaled, WIDE, axis=0, tiled=True),
-        lax.all_gather(low_dir, WIDE, axis=0, tiled=True),
+        jnp.concatenate(
+            lax.all_to_all(jnp.stack([low_dir] * lax.axis_size(WIDE)), WIDE, 0, 0), axis=0
+        ),
     )
     block_sq = squares_of(block_x)
     cycle_size = lax.axis_size(BLK)

time: 303 us -> 291 us (0.960)
  waiting for transfers between devices: 43.9 us -> 21.1 us
  between operations: 14.8 us -> 1.41 us
  blocking collectives: 133 us -> 143 us
  starting transfers between devices: 47.4 us -> 57.2 us
  matrix products: 47.5 us -> 55.4 us
    all_gather x1 -> x0, waiting for transfers between devices: 22.2 us -> none  [on_device(): lax.all_gather(low_dir, WIDE, axis=0, tiled=True)]
    all_to_all x0 -> x1, starting transfers between devices: none -> 10.3 us  [on_device(): lax.all_to_all(jnp.stack([low_dir] * lax.axis_size(WIDE)), WIDE, 0, 0)]
    all_gather x1, blocking collectives: 50.2 us -> 59.9 us  [on_device(): lax.all_gather(scaled, WIDE, axis=0, tiled=True)]
    dot_general x7, matrix products: 21.6 us -> 28.6 us  [kernel_tile(): lax.dot_general(rows_x, cols_x, (((1,), (1,)), ((), ())), preferred_eleme...]
    while x28 -> x14, local copies, waits for them, and re-layouts: 7.39 us -> 4.47 us
  transfers between devices with their start and end apart: 26 -> 26, of which waited for: 4 -> 3; matrix products, arithmetic and copies ran while one was open for 13% -> 16% of each run, Pallas kernels for 0% -> 0%
where the time goes in v1:
time: 291 us
  blocking collectives  143 us (49%)
  starting transfers between devices  57.2 us (20%)
  matrix products  55.4 us (19%)
  waiting for transfers between devices  21.1 us (7%)
  local copies, waits for them, and re-layouts  6.84 us (2%)
  other arithmetic  5.42 us (2%)
    psum x10, blocking collectives, over_axes(): return functools.reduce(lax.psum, axes, x)  82.8 us
    all_gather x1, blocking collectives, on_device(): lax.all_gather(scaled, WIDE, axis=0, tiled=True)  59.9 us
    ppermute x24, starting transfers between devices, shifted(): return lax.ppermute(x, axis, [(i, (i + by) % count) for i in range(count)])  43.1 us
    dot_general x7, matrix products, kernel_tile(): lax.dot_general(rows_x, cols_x, (((1,), (1,)), ((), ())), preferred_eleme...  28.6 us
    all_to_all x1, waiting for transfers between devices, sent_and_summed(): blocks = lax.all_to_all(cut_along(x, dim, count), axis, 0, 0, tiled=True)  19.3 us
    dot_general x7, matrix products, paired_turn(): lax.dot_general(kernel_block, block_p, (((0,), (0,)), ((), ())), preferre...  11.8 us
    all_to_all x1, starting transfers between devices, on_device(): lax.all_to_all(jnp.stack([low_dir] * lax.axis_size(WIDE)), WIDE, 0, 0)  10.3 us
  transfers between devices with their start and end apart: 26, of which 3 were waited for; matrix products, arithmetic and copies ran while one was open for 16% of the time, Pallas kernels for 0%

profile of v1, /device:TPU:10, one launch (start us, length us, event | category | flops | bytes accessed | tf_op | source)
XLA Modules:
  0.0 290.6 jit_solution(9810439706259020392)
XLA Ops:
  1.6 1.2 stack.2
  2.8 10.3 %all-to-all-start = ((bf16[16,256,128]{2,1,0:T(8,128)(2,1)}), bf16[16,256,128]{2,1,0:T(8,128)(2,1)S(1)}, u32[]{:S(2)}, u32[]{:S(2)}) async-start(bf16[16,256,128]{2,1,0:T(8,128)(2,1)} %stack.2), calls=%async_computation | async-start | bytes 2097152 | tf_op jit(solution)/shard_map/all_to_all | solution.py:54
  13.1 2.2 collective-permute-start.4
  16.1 1.4 collective-permute-start.3
  17.5 59.9 %all_gather.3 = bf16[4096,32]{1,0:T(8,128)(2,1)S(1)} all-gather(bf16[256,32]{1,0:T(8,128)(2,1)} %get-tuple-element.156), channel_id=1, replica_groups=mesh['blk_0'=4,'blk_1'=2,'blk_2'=2,'wide_0'=2,'wide_1'=8] {'wide_0','wid..., dimensions={0}, use_global_device_ids=true | all-gather | bytes 278528 | tf_op jit(solution)/shard_map/all_gather | solution.py:52
  78.5 4.2 %fusion.5 = f32[4096,128]{1,0:T(8,128)S(1)} fusion(bf16[256,128]{1,0:T(8,128)(2,1)S(1)} %convert_element_type.38, bf16[4096,32]{1,0:T(8,128)(2,1)} %copy-done, bf16[256,32]{1,0:T(8,128)(2,1)} %get-tuple-element.156, f32[256]{0:T(256)S(1)} %get-tuple-element.103, f32[4096]{0:T(1024)S(1)} %multiply_reduce_fusion.1), kind=kOutput, calls=%fused_computation.18 | convolution fusion | flops 348127232 | bytes 2458624 | tf_op jit(solution)/shard_map/dot_general | solution.py:61
  84.0 83.4 %while.17 = (s32[]{:T(128)}, bf16[256,32]{1,0:T(8,128)(2,1)}, bf16[256,128]{1,0:T(8,128)(2,1)S(1)}, f32[256,128]{1,0:T(8,128)S(1)}, f32[4096,128]{1,0:T(8,128)S(...) while((s32[]{:T(128)}, bf16[256,32]{1,0:T(8,128)(2,1)}, ...), condition=%wide.region_10.0_spmd.clone, body=%wide.region_8.10_spmd.clone.sunk | while | flops 617176832 | bytes 13453543 | solution.py:76
  84.0 2.5 collective-permute-start.2
  86.6 1.3 collective-permute-done
  88.0 4.1 %multiply_convert_fusion.6 = bf16[4096,256]{1,0:T(8,128)(2,1)S(1)} fusion(bf16[4096,32]{1,0:T(8,128)(2,1)} %get-tuple-element.181, bf16[256,32]{1,0:T(8,128)(2,1)S(1)} %collective-permute-done, f32[256]{0:T(256)S(1)} %multiply_reduce_fusion.8, f32[4096]{0:T(1024)S(1)} %get-tuple-element.180), kind=kOutput, calls=%fused_computation.2.clone.1 | convolution fusion | flops 79691776 | bytes 2393088 | tf_op jit(solution)/shard_map/while/body/eval_jaxpr/dot_general | solution.py:39
  93.6 1.7 convolution_add_fusion.5
  95.5 3.2 %collective-permute-start.2 = (f32[256,128]{1,0:T(8,128)S(1)}, f32[256,128]{1,0:T(8,128)}, u32[]{:S(2)}, u32[]{:S(2)}) collective-permute-start(f32[256,128]{1,0:T(8,128)S(1)} %broadcast_select_fusion.2), channel_id=1, source_target_pairs={{0,16},{16,32},{32,48},{48,64},{64,80},{80,96},{96,112},{112,128},... | collective-permute-start | bytes 393224 | tf_op jit(solution)/shard_map/while/body/eval_jaxpr/ppermute | solution.py:15
  99.4 4.1 %multiply_convert_fusion.6 = bf16[4096,256]{1,0:T(8,128)(2,1)S(1)} fusion(bf16[4096,32]{1,0:T(8,128)(2,1)} %get-tuple-element.181, bf16[256,32]{1,0:T(8,128)(2,1)S(1)} %collective-permute-done, f32[256]{0:T(256)S(1)} %multiply_reduce_fusion.8, f32[4096]{0:T(1024)S(1)} %get-tuple-element.180), kind=kOutput, calls=%fused_computation.2.clone.1 | convolution fusion | flops 79691776 | bytes 2393088 | tf_op jit(solution)/shard_map/while/body/eval_jaxpr/dot_general | solution.py:39
  104.9 1.7 convolution_add_fusion.5
  106.6 1.1 collective-permute-start
  107.8 3.2 %collective-permute-start.2 = (f32[256,128]{1,0:T(8,128)S(1)}, f32[256,128]{1,0:T(8,128)}, u32[]{:S(2)}, u32[]{:S(2)}) collective-permute-start(f32[256,128]{1,0:T(8,128)S(1)} %broadcast_select_fusion.2), channel_id=1, source_target_pairs={{0,16},{16,32},{32,48},{48,64},{64,80},{80,96},{96,112},{112,128},... | collective-permute-start | bytes 393224 | tf_op jit(solution)/shard_map/while/body/eval_jaxpr/ppermute | solution.py:15
  111.2 4.1 %multiply_convert_fusion.6 = bf16[4096,256]{1,0:T(8,128)(2,1)S(1)} fusion(bf16[4096,32]{1,0:T(8,128)(2,1)} %get-tuple-element.181, bf16[256,32]{1,0:T(8,128)(2,1)S(1)} %collective-permute-done, f32[256]{0:T(256)S(1)} %multiply_reduce_fusion.8, f32[4096]{0:T(1024)S(1)} %get-tuple-element.180), kind=kOutput, calls=%fused_computation.2.clone.1 | convolution fusion | flops 79691776 | bytes 2393088 | tf_op jit(solution)/shard_map/while/body/eval_jaxpr/dot_general | solution.py:39
  116.7 1.7 convolution_add_fusion.5
  118.4 1.5 collective-permute-start
  120.0 3.2 %collective-permute-start.2 = (f32[256,128]{1,0:T(8,128)S(1)}, f32[256,128]{1,0:T(8,128)}, u32[]{:S(2)}, u32[]{:S(2)}) collective-permute-start(f32[256,128]{1,0:T(8,128)S(1)} %broadcast_select_fusion.2), channel_id=1, source_target_pairs={{0,16},{16,32},{32,48},{48,64},{64,80},{80,96},{96,112},{112,128},... | collective-permute-start | bytes 393224 | tf_op jit(solution)/shard_map/while/body/eval_jaxpr/ppermute | solution.py:15
  123.4 4.1 %multiply_convert_fusion.6 = bf16[4096,256]{1,0:T(8,128)(2,1)S(1)} fusion(bf16[4096,32]{1,0:T(8,128)(2,1)} %get-tuple-element.181, bf16[256,32]{1,0:T(8,128)(2,1)S(1)} %collective-permute-done, f32[256]{0:T(256)S(1)} %multiply_reduce_fusion.8, f32[4096]{0:T(1024)S(1)} %get-tuple-element.180), kind=kOutput, calls=%fused_computation.2.clone.1 | convolution fusion | flops 79691776 | bytes 2393088 | tf_op jit(solution)/shard_map/while/body/eval_jaxpr/dot_general | solution.py:39
  129.0 1.7 convolution_add_fusion.5
  130.7 1.5 collective-permute-start
  132.2 3.2 %collective-permute-start.2 = (f32[256,128]{1,0:T(8,128)S(1)}, f32[256,128]{1,0:T(8,128)}, u32[]{:S(2)}, u32[]{:S(2)}) collective-permute-start(f32[256,128]{1,0:T(8,128)S(1)} %broadcast_select_fusion.2), channel_id=1, source_target_pairs={{0,16},{16,32},{32,48},{48,64},{64,80},{80,96},{96,112},{112,128},... | collective-permute-start | bytes 393224 | tf_op jit(solution)/shard_map/while/body/eval_jaxpr/ppermute | solution.py:15
  135.7 4.1 %multiply_convert_fusion.6 = bf16[4096,256]{1,0:T(8,128)(2,1)S(1)} fusion(bf16[4096,32]{1,0:T(8,128)(2,1)} %get-tuple-element.181, bf16[256,32]{1,0:T(8,128)(2,1)S(1)} %collective-permute-done, f32[256]{0:T(256)S(1)} %multiply_reduce_fusion.8, f32[4096]{0:T(1024)S(1)} %get-tuple-element.180), kind=kOutput, calls=%fused_computation.2.clone.1 | convolution fusion | flops 79691776 | bytes 2393088 | tf_op jit(solution)/shard_map/while/body/eval_jaxpr/dot_general | solution.py:39
  141.2 1.7 convolution_add_fusion.5
  142.9 1.5 collective-permute-start
  144.5 3.2 %collective-permute-start.2 = (f32[256,128]{1,0:T(8,128)S(1)}, f32[256,128]{1,0:T(8,128)}, u32[]{:S(2)}, u32[]{:S(2)}) collective-permute-start(f32[256,128]{1,0:T(8,128)S(1)} %broadcast_select_fusion.2), channel_id=1, source_target_pairs={{0,16},{16,32},{32,48},{48,64},{64,80},{80,96},{96,112},{112,128},... | collective-permute-start | bytes 393224 | tf_op jit(solution)/shard_map/while/body/eval_jaxpr/ppermute | solution.py:15
  147.9 4.1 %multiply_convert_fusion.6 = bf16[4096,256]{1,0:T(8,128)(2,1)S(1)} fusion(bf16[4096,32]{1,0:T(8,128)(2,1)} %get-tuple-element.181, bf16[256,32]{1,0:T(8,128)(2,1)S(1)} %collective-permute-done, f32[256]{0:T(256)S(1)} %multiply_reduce_fusion.8, f32[4096]{0:T(1024)S(1)} %get-tuple-element.180), kind=kOutput, calls=%fused_computation.2.clone.1 | convolution fusion | flops 79691776 | bytes 2393088 | tf_op jit(solution)/shard_map/while/body/eval_jaxpr/dot_general | solution.py:39
  153.4 1.7 convolution_add_fusion.5
  155.1 1.5 collective-permute-start
  156.7 3.2 %collective-permute-start.2 = (f32[256,128]{1,0:T(8,128)S(1)}, f32[256,128]{1,0:T(8,128)}, u32[]{:S(2)}, u32[]{:S(2)}) collective-permute-start(f32[256,128]{1,0:T(8,128)S(1)} %broadcast_select_fusion.2), channel_id=1, source_target_pairs={{0,16},{16,32},{32,48},{48,64},{64,80},{80,96},{96,112},{112,128},... | collective-permute-start | bytes 393224 | tf_op jit(solution)/shard_map/while/body/eval_jaxpr/ppermute | solution.py:15
  160.1 4.1 %multiply_convert_fusion.6 = bf16[4096,256]{1,0:T(8,128)(2,1)S(1)} fusion(bf16[4096,32]{1,0:T(8,128)(2,1)} %get-tuple-element.181, bf16[256,32]{1,0:T(8,128)(2,1)S(1)} %collective-permute-done, f32[256]{0:T(256)S(1)} %multiply_reduce_fusion.8, f32[4096]{0:T(1024)S(1)} %get-tuple-element.180), kind=kOutput, calls=%fused_computation.2.clone.1 | convolution fusion | flops 79691776 | bytes 2393088 | tf_op jit(solution)/shard_map/while/body/eval_jaxpr/dot_general | solution.py:39
  165.7 1.7 convolution_add_fusion.5
  167.4 5.4 %fusion.4 = bf16[4096,128]{1,0:T(8,128)(2,1)} fusion(f32[4096,128]{1,0:T(8,128)S(1)} %get-tuple-element.46, bf16[256,128]{1,0:T(8,128)(2,1)} %copy-done.8, f32[256]{0:T(256)} %multiply_reduce_fusion.4, bf16[4096,32]{1,0:T(8,128)(2,1)} %get-tuple-element.188, bf16[256,32]{1,0:T(8,128)(2,1)} %copy-done.5, f32[4096]{0:T(1024)S(1)} %get-tuple-element.198), kind=kOutput, calls=%fused_computation.13 | convolution fusion | flops 349175808 | bytes 3507200 | tf_op jit(solution)/shard_map/dot_general | solution.py:80
  172.8 3.8 %all-to-all-start.1 = ((bf16[16,256,128]{2,1,0:T(8,128)(2,1)}), bf16[16,256,128]{2,1,0:T(8,128)(2,1)S(1)}, u32[]{:S(2)}, u32[]{:S(2)}) async-start(bf16[16,256,128]{2,1,0:T(8,128)(2,1)} %bitcast.27), calls=%async_computation.1 | async-start | bytes 2097152 | tf_op jit(solution)/shard_map/all_to_all | solution.py:25
  177.3 9.5 %collective-permute-start.5 = (f32[256,128]{1,0:T(8,128)S(1)}, f32[256,128]{1,0:T(8,128)S(1)}, u32[]{:S(2)}, u32[]{:S(2)}) collective-permute-start(f32[256,128]{1,0:T(8,128)S(1)} %get-tuple-element.47), channel_id=1, source_target_pairs={{0,144},{16,160},{32,176},{48,192},{64,208},{80,224},{96,240},{112... | collective-permute-start | bytes 393224 | tf_op jit(solution)/shard_map/ppermute | solution.py:15
  186.8 19.3 %all-to-all-done.1 = bf16[16,256,128]{2,1,0:T(8,128)(2,1)S(1)} async-done(((bf16[16,256,128]{2,1,0:T(8,128)(2,1)}), bf16[16,256,128]{2,1,0:T(8,128)(2,1)S(1)}, u32[]{:S(2)}, u32[]{:S(2)}) %all-to-all-start.1) | async-done | bytes 1048608 | tf_op jit(solution)/shard_map/all_to_all | solution.py:25
  206.3 14.0 %all-reduce.1 = (f32[128]{0:T(128)S(1)}, f32[128]{0:T(128)S(1)}) all-reduce(f32[128]{0:T(128)S(1)} %multiply_reduce_fusion.6, f32[128]{0:T(128)S(1)} %multiply_reduce_fusion.3), channel_id=1, replica_groups=mesh['blk_0'=4,'blk_1'=2,'blk_2'=2,'wide_0'=2,'wide_1'=8] {'blk_0'}, use_global_device_ids=true, to_apply=%region_1.0 | all-reduce | flops 256 | bytes 2048 | tf_op jit(solution)/shard_map/psum | solution.py:30
  220.4 4.9 %all-reduce.4 = (f32[128]{0:T(128)S(1)}, f32[128]{0:T(128)S(1)}) all-reduce(f32[128]{0:T(128)S(1)} %get-tuple-element.93, f32[128]{0:T(128)S(1)} %get-tuple-element.94), channel_id=1, replica_groups=mesh['blk_0'=4,'blk_1'=2,'blk_2'=2,'wide_0'=2,'wide_1'=8] {'blk_1'}, use_global_device_ids=true, to_apply=%region_2.3 | all-reduce | flops 256 | bytes 2048 | tf_op jit(solution)/shard_map/psum | solution.py:30
  225.3 2.4 all-reduce.3
  227.7 6.4 %all-reduce.2 = (f32[128]{0:T(128)S(1)}, f32[128]{0:T(128)S(1)}) all-reduce(f32[128]{0:T(128)S(1)} %get-tuple-element.97, f32[128]{0:T(128)S(1)} %get-tuple-element.98), channel_id=1, replica_groups=mesh['blk_0'=4,'blk_1'=2,'blk_2'=2,'wide_0'=2,'wide_1'=8] {'wide_0'}, use_global_device_ids=true, to_apply=%region_4.0 | all-reduce | flops 256 | bytes 2048 | tf_op jit(solution)/shard_map/psum | solution.py:30
  234.2 15.1 %all-reduce = (f32[128]{0:T(128)S(1)}, f32[128]{0:T(128)S(1)}) all-reduce(f32[128]{0:T(128)S(1)} %get-tuple-element.95, f32[128]{0:T(128)S(1)} %get-tuple-element.96), channel_id=1, replica_groups=mesh['blk_0'=4,'blk_1'=2,'blk_2'=2,'wide_0'=2,'wide_1'=8] {'wide_1'}, use_global_device_ids=true, to_apply=%region_5.0 | all-reduce | flops 256 | bytes 2048 | tf_op jit(solution)/shard_map/psum | solution.py:30
  250.0 10.9 %psum.115 = f32[128]{0:T(128)S(1)} all-reduce(f32[128]{0:T(128)S(1)} %get-tuple-element.101), channel_id=1, replica_groups=mesh['blk_0'=4,'blk_1'=2,'blk_2'=2,'wide_0'=2,'wide_1'=8] {'blk_0'}, use_global_device_ids=true, to_apply=%region_20.0 | all-reduce | flops 128 | bytes 1024 | tf_op jit(solution)/shard_map/psum | solution.py:30
  260.9 4.9 %psum.116 = f32[128]{0:T(128)S(1)} all-reduce(f32[128]{0:T(128)S(1)} %psum.115), channel_id=1, replica_groups=mesh['blk_0'=4,'blk_1'=2,'blk_2'=2,'wide_0'=2,'wide_1'=8] {'blk_1'}, use_global_device_ids=true, to_apply=%region_21.0 | all-reduce | flops 128 | bytes 1024 | tf_op jit(solution)/shard_map/psum | solution.py:30
  265.8 2.4 psum.117
  268.3 6.4 %psum.118 = f32[128]{0:T(128)S(1)} all-reduce(f32[128]{0:T(128)S(1)} %psum.117), channel_id=1, replica_groups=mesh['blk_0'=4,'blk_1'=2,'blk_2'=2,'wide_0'=2,'wide_1'=8] {'wide_0'}, use_global_device_ids=true, to_apply=%region_23.0 | all-reduce | flops 128 | bytes 1024 | tf_op jit(solution)/shard_map/psum | solution.py:30
  274.7 15.2 %psum.119 = f32[128]{0:T(128)S(1)} all-reduce(f32[128]{0:T(128)S(1)} %psum.118), channel_id=1, replica_groups=mesh['blk_0'=4,'blk_1'=2,'blk_2'=2,'wide_0'=2,'wide_1'=8] {'wide_1'}, use_global_device_ids=true, to_apply=%region_24.0 | all-reduce | flops 128 | bytes 1024 | tf_op jit(solution)/shard_map/psum | solution.py:30
  (99 shorter events, 17.8 us)
Async XLA Ops:
  0.6 14.7 %copy-start.6 = (bf16[256,32]{0,1:T(8,128)(2,1)S(1)}, bf16[256,32]{0,1:T(8,128)(2,1)}, u32[]{:S(2)}) copy-start(bf16[256,32]{0,1:T(8,128)(2,1)} %param.8) | copy-start | bytes 49156
  0.6 14.8 %copy-start.7 = (f32[32]{0:T(128)S(1)}, f32[32]{0:T(128)}, u32[]{:S(2)}) copy-start(f32[32]{0:T(128)} %param.9) | copy-start | bytes 388
  2.8 80.6 %all-to-all-start = ((bf16[16,256,128]{2,1,0:T(8,128)(2,1)}), bf16[16,256,128]{2,1,0:T(8,128)(2,1)S(1)}, u32[]{:S(2)}, u32[]{:S(2)}) async-start(bf16[16,256,128]{2,1,0:T(8,128)(2,1)} %stack.2), calls=%async_computation | async-start | bytes 2097152 | tf_op jit(solution)/shard_map/all_to_all | solution.py:54
  13.1 70.3 %collective-permute-start.4 = (bf16[256,128]{1,0:T(8,128)(2,1)S(1)}, bf16[256,128]{1,0:T(8,128)(2,1)S(1)}, u32[]{:S(2)}, u32[]{:S(2)}) collective-permute-start(bf16[256,128]{1,0:T(8,128)(2,1)S(1)} %convert_element_type.38), channel_id=1, source_target_pairs={{0,128},{16,144},{32,160},{48,176},{64,192},{80,208},{96,224},{112... | collective-permute-start | bytes 196616 | tf_op jit(solution)/shard_map/ppermute | solution.py:15
  16.1 66.5 %collective-permute-start.3 = (bf16[256,32]{1,0:T(8,128)(2,1)}, bf16[256,32]{1,0:T(8,128)(2,1)S(1)}, u32[]{:S(2)}, u32[]{:S(2)}) collective-permute-start(bf16[256,32]{1,0:T(8,128)(2,1)} %get-tuple-element.156), channel_id=1, source_target_pairs={{0,128},{16,144},{32,160},{48,176},{64,192},{80,208},{96,224},{112... | collective-permute-start | bytes 49160 | tf_op jit(solution)/shard_map/ppermute | solution.py:15
  77.5 1.0 copy-start
  82.7 0.7 copy-start.5
  83.4 0.6 copy-start.8
  84.0 3.9 %collective-permute-start = (bf16[256,32]{1,0:T(8,128)(2,1)}, bf16[256,32]{1,0:T(8,128)(2,1)S(1)}, u32[]{:S(2)}, u32[]{:S(2)}) collective-permute-start(bf16[256,32]{1,0:T(8,128)(2,1)} %get-tuple-element.166), channel_id=1, source_target_pairs={{0,16},{16,32},{32,48},{48,64},{64,80},{80,96},{96,112},{112,128},... | collective-permute-start | bytes 49160 | tf_op jit(solution)/shard_map/while/body/eval_jaxpr/ppermute | solution.py:15
  84.0 9.5 %collective-permute-start.2 = (f32[256,128]{1,0:T(8,128)S(1)}, f32[256,128]{1,0:T(8,128)}, u32[]{:S(2)}, u32[]{:S(2)}) collective-permute-start(f32[256,128]{1,0:T(8,128)S(1)} %broadcast_select_fusion.2), channel_id=1, source_target_pairs={{0,16},{16,32},{32,48},{48,64},{64,80},{80,96},{96,112},{112,128},... | collective-permute-start | bytes 393224 | tf_op jit(solution)/shard_map/while/body/eval_jaxpr/ppermute | solution.py:15
  86.5 6.3 %collective-permute-start.1 = (bf16[256,128]{1,0:T(8,128)(2,1)S(1)}, bf16[256,128]{1,0:T(8,128)(2,1)S(1)}, u32[]{:S(2)}, u32[]{:S(2)}) collective-permute-start(bf16[256,128]{1,0:T(8,128)(2,1)S(1)} %get-tuple-element.167), channel_id=1, source_target_pairs={{0,16},{16,32},{32,48},{48,64},{64,80},{80,96},{96,112},{112,128},... | collective-permute-start | bytes 196616 | tf_op jit(solution)/shard_map/while/body/eval_jaxpr/ppermute | solution.py:15
  95.3 4.0 %collective-permute-start = (bf16[256,32]{1,0:T(8,128)(2,1)}, bf16[256,32]{1,0:T(8,128)(2,1)S(1)}, u32[]{:S(2)}, u32[]{:S(2)}) collective-permute-start(bf16[256,32]{1,0:T(8,128)(2,1)} %get-tuple-element.166), channel_id=1, source_target_pairs={{0,16},{16,32},{32,48},{48,64},{64,80},{80,96},{96,112},{112,128},... | collective-permute-start | bytes 49160 | tf_op jit(solution)/shard_map/while/body/eval_jaxpr/ppermute | solution.py:15
  95.5 9.4 %collective-permute-start.2 = (f32[256,128]{1,0:T(8,128)S(1)}, f32[256,128]{1,0:T(8,128)}, u32[]{:S(2)}, u32[]{:S(2)}) collective-permute-start(f32[256,128]{1,0:T(8,128)S(1)} %broadcast_select_fusion.2), channel_id=1, source_target_pairs={{0,16},{16,32},{32,48},{48,64},{64,80},{80,96},{96,112},{112,128},... | collective-permute-start | bytes 393224 | tf_op jit(solution)/shard_map/while/body/eval_jaxpr/ppermute | solution.py:15
  98.7 5.4 %collective-permute-start.1 = (bf16[256,128]{1,0:T(8,128)(2,1)S(1)}, bf16[256,128]{1,0:T(8,128)(2,1)S(1)}, u32[]{:S(2)}, u32[]{:S(2)}) collective-permute-start(bf16[256,128]{1,0:T(8,128)(2,1)S(1)} %get-tuple-element.167), channel_id=1, source_target_pairs={{0,16},{16,32},{32,48},{48,64},{64,80},{80,96},{96,112},{112,128},... | collective-permute-start | bytes 196616 | tf_op jit(solution)/shard_map/while/body/eval_jaxpr/ppermute | solution.py:15
  106.6 4.4 %collective-permute-start = (bf16[256,32]{1,0:T(8,128)(2,1)}, bf16[256,32]{1,0:T(8,128)(2,1)S(1)}, u32[]{:S(2)}, u32[]{:S(2)}) collective-permute-start(bf16[256,32]{1,0:T(8,128)(2,1)} %get-tuple-element.166), channel_id=1, source_target_pairs={{0,16},{16,32},{32,48},{48,64},{64,80},{80,96},{96,112},{112,128},... | collective-permute-start | bytes 49160 | tf_op jit(solution)/shard_map/while/body/eval_jaxpr/ppermute | solution.py:15
  107.8 9.0 %collective-permute-start.2 = (f32[256,128]{1,0:T(8,128)S(1)}, f32[256,128]{1,0:T(8,128)}, u32[]{:S(2)}, u32[]{:S(2)}) collective-permute-start(f32[256,128]{1,0:T(8,128)S(1)} %broadcast_select_fusion.2), channel_id=1, source_target_pairs={{0,16},{16,32},{32,48},{48,64},{64,80},{80,96},{96,112},{112,128},... | collective-permute-start | bytes 393224 | tf_op jit(solution)/shard_map/while/body/eval_jaxpr/ppermute | solution.py:15
  111.0 4.9 %collective-permute-start.1 = (bf16[256,128]{1,0:T(8,128)(2,1)S(1)}, bf16[256,128]{1,0:T(8,128)(2,1)S(1)}, u32[]{:S(2)}, u32[]{:S(2)}) collective-permute-start(bf16[256,128]{1,0:T(8,128)(2,1)S(1)} %get-tuple-element.167), channel_id=1, source_target_pairs={{0,16},{16,32},{32,48},{48,64},{64,80},{80,96},{96,112},{112,128},... | collective-permute-start | bytes 196616 | tf_op jit(solution)/shard_map/while/body/eval_jaxpr/ppermute | solution.py:15
  118.4 4.9 %collective-permute-start = (bf16[256,32]{1,0:T(8,128)(2,1)}, bf16[256,32]{1,0:T(8,128)(2,1)S(1)}, u32[]{:S(2)}, u32[]{:S(2)}) collective-permute-start(bf16[256,32]{1,0:T(8,128)(2,1)} %get-tuple-element.166), channel_id=1, source_target_pairs={{0,16},{16,32},{32,48},{48,64},{64,80},{80,96},{96,112},{112,128},... | collective-permute-start | bytes 49160 | tf_op jit(solution)/shard_map/while/body/eval_jaxpr/ppermute | solution.py:15
  120.0 9.0 %collective-permute-start.2 = (f32[256,128]{1,0:T(8,128)S(1)}, f32[256,128]{1,0:T(8,128)}, u32[]{:S(2)}, u32[]{:S(2)}) collective-permute-start(f32[256,128]{1,0:T(8,128)S(1)} %broadcast_select_fusion.2), channel_id=1, source_target_pairs={{0,16},{16,32},{32,48},{48,64},{64,80},{80,96},{96,112},{112,128},... | collective-permute-start | bytes 393224 | tf_op jit(solution)/shard_map/while/body/eval_jaxpr/ppermute | solution.py:15
  123.2 4.9 %collective-permute-start.1 = (bf16[256,128]{1,0:T(8,128)(2,1)S(1)}, bf16[256,128]{1,0:T(8,128)(2,1)S(1)}, u32[]{:S(2)}, u32[]{:S(2)}) collective-permute-start(bf16[256,128]{1,0:T(8,128)(2,1)S(1)} %get-tuple-element.167), channel_id=1, source_target_pairs={{0,16},{16,32},{32,48},{48,64},{64,80},{80,96},{96,112},{112,128},... | collective-permute-start | bytes 196616 | tf_op jit(solution)/shard_map/while/body/eval_jaxpr/ppermute | solution.py:15
  130.7 4.9 %collective-permute-start = (bf16[256,32]{1,0:T(8,128)(2,1)}, bf16[256,32]{1,0:T(8,128)(2,1)S(1)}, u32[]{:S(2)}, u32[]{:S(2)}) collective-permute-start(bf16[256,32]{1,0:T(8,128)(2,1)} %get-tuple-element.166), channel_id=1, source_target_pairs={{0,16},{16,32},{32,48},{48,64},{64,80},{80,96},{96,112},{112,128},... | collective-permute-start | bytes 49160 | tf_op jit(solution)/shard_map/while/body/eval_jaxpr/ppermute | solution.py:15
  132.2 9.0 %collective-permute-start.2 = (f32[256,128]{1,0:T(8,128)S(1)}, f32[256,128]{1,0:T(8,128)}, u32[]{:S(2)}, u32[]{:S(2)}) collective-permute-start(f32[256,128]{1,0:T(8,128)S(1)} %broadcast_select_fusion.2), channel_id=1, source_target_pairs={{0,16},{16,32},{32,48},{48,64},{64,80},{80,96},{96,112},{112,128},... | collective-permute-start | bytes 393224 | tf_op jit(solution)/shard_map/while/body/eval_jaxpr/ppermute | solution.py:15
  135.5 4.9 %collective-permute-start.1 = (bf16[256,128]{1,0:T(8,128)(2,1)S(1)}, bf16[256,128]{1,0:T(8,128)(2,1)S(1)}, u32[]{:S(2)}, u32[]{:S(2)}) collective-permute-start(bf16[256,128]{1,0:T(8,128)(2,1)S(1)} %get-tuple-element.167), channel_id=1, source_target_pairs={{0,16},{16,32},{32,48},{48,64},{64,80},{80,96},{96,112},{112,128},... | collective-permute-start | bytes 196616 | tf_op jit(solution)/shard_map/while/body/eval_jaxpr/ppermute | solution.py:15
  142.9 4.9 %collective-permute-start = (bf16[256,32]{1,0:T(8,128)(2,1)}, bf16[256,32]{1,0:T(8,128)(2,1)S(1)}, u32[]{:S(2)}, u32[]{:S(2)}) collective-permute-start(bf16[256,32]{1,0:T(8,128)(2,1)} %get-tuple-element.166), channel_id=1, source_target_pairs={{0,16},{16,32},{32,48},{48,64},{64,80},{80,96},{96,112},{112,128},... | collective-permute-start | bytes 49160 | tf_op jit(solution)/shard_map/while/body/eval_jaxpr/ppermute | solution.py:15
  144.5 9.0 %collective-permute-start.2 = (f32[256,128]{1,0:T(8,128)S(1)}, f32[256,128]{1,0:T(8,128)}, u32[]{:S(2)}, u32[]{:S(2)}) collective-permute-start(f32[256,128]{1,0:T(8,128)S(1)} %broadcast_select_fusion.2), channel_id=1, source_target_pairs={{0,16},{16,32},{32,48},{48,64},{64,80},{80,96},{96,112},{112,128},... | collective-permute-start | bytes 393224 | tf_op jit(solution)/shard_map/while/body/eval_jaxpr/ppermute | solution.py:15
  147.7 4.9 %collective-permute-start.1 = (bf16[256,128]{1,0:T(8,128)(2,1)S(1)}, bf16[256,128]{1,0:T(8,128)(2,1)S(1)}, u32[]{:S(2)}, u32[]{:S(2)}) collective-permute-start(bf16[256,128]{1,0:T(8,128)(2,1)S(1)} %get-tuple-element.167), channel_id=1, source_target_pairs={{0,16},{16,32},{32,48},{48,64},{64,80},{80,96},{96,112},{112,128},... | collective-permute-start | bytes 196616 | tf_op jit(solution)/shard_map/while/body/eval_jaxpr/ppermute | solution.py:15
  155.1 4.9 %collective-permute-start = (bf16[256,32]{1,0:T(8,128)(2,1)}, bf16[256,32]{1,0:T(8,128)(2,1)S(1)}, u32[]{:S(2)}, u32[]{:S(2)}) collective-permute-start(bf16[256,32]{1,0:T(8,128)(2,1)} %get-tuple-element.166), channel_id=1, source_target_pairs={{0,16},{16,32},{32,48},{48,64},{64,80},{80,96},{96,112},{112,128},... | collective-permute-start | bytes 49160 | tf_op jit(solution)/shard_map/while/body/eval_jaxpr/ppermute | solution.py:15
  156.7 9.0 %collective-permute-start.2 = (f32[256,128]{1,0:T(8,128)S(1)}, f32[256,128]{1,0:T(8,128)}, u32[]{:S(2)}, u32[]{:S(2)}) collective-permute-start(f32[256,128]{1,0:T(8,128)S(1)} %broadcast_select_fusion.2), channel_id=1, source_target_pairs={{0,16},{16,32},{32,48},{48,64},{64,80},{80,96},{96,112},{112,128},... | collective-permute-start | bytes 393224 | tf_op jit(solution)/shard_map/while/body/eval_jaxpr/ppermute | solution.py:15
  159.9 4.9 %collective-permute-start.1 = (bf16[256,128]{1,0:T(8,128)(2,1)S(1)}, bf16[256,128]{1,0:T(8,128)(2,1)S(1)}, u32[]{:S(2)}, u32[]{:S(2)}) collective-permute-start(bf16[256,128]{1,0:T(8,128)(2,1)S(1)} %get-tuple-element.167), channel_id=1, source_target_pairs={{0,16},{16,32},{32,48},{48,64},{64,80},{80,96},{96,112},{112,128},... | collective-permute-start | bytes 196616 | tf_op jit(solution)/shard_map/while/body/eval_jaxpr/ppermute | solution.py:15
  172.8 4.5 %copy-start.2 = (f32[256,128]{1,0:T(8,128)S(1)}, f32[256,128]{1,0:T(8,128)}, u32[]{:S(2)}) copy-start(f32[256,128]{1,0:T(8,128)} %param.12) | copy-start | bytes 393220
  172.8 33.5 %copy-start.1 = (f32[256,128]{1,0:T(8,128)S(1)}, f32[256,128]{1,0:T(8,128)}, u32[]{:S(2)}) copy-start(f32[256,128]{1,0:T(8,128)} %param.13) | copy-start | bytes 393220
  172.8 76.5 %copy-start.4 = (f32[256,128]{1,0:T(8,128)S(1)}, f32[256,128]{1,0:T(8,128)}, u32[]{:S(2)}) copy-start(f32[256,128]{1,0:T(8,128)} %param.11) | copy-start | bytes 393220
  172.8 33.3 %all-to-all-start.1 = ((bf16[16,256,128]{2,1,0:T(8,128)(2,1)}), bf16[16,256,128]{2,1,0:T(8,128)(2,1)S(1)}, u32[]{:S(2)}, u32[]{:S(2)}) async-start(bf16[16,256,128]{2,1,0:T(8,128)(2,1)} %bitcast.27), calls=%async_computation.1 | async-start | bytes 2097152 | tf_op jit(solution)/shard_map/all_to_all | solution.py:25
  177.3 29.0 %collective-permute-start.5 = (f32[256,128]{1,0:T(8,128)S(1)}, f32[256,128]{1,0:T(8,128)S(1)}, u32[]{:S(2)}, u32[]{:S(2)}) collective-permute-start(f32[256,128]{1,0:T(8,128)S(1)} %get-tuple-element.47), channel_id=1, source_target_pairs={{0,144},{16,160},{32,176},{48,192},{64,208},{80,224},{96,240},{112... | collective-permute-start | bytes 393224 | tf_op jit(solution)/shard_map/ppermute | solution.py:15
  250.0 40.6 %copy-start.3 = (f32[256,128]{1,0:T(8,128)}, f32[256,128]{1,0:T(8,128)S(1)}, u32[]{:S(2)}) copy-start(f32[256,128]{1,0:T(8,128)S(1)} %get-tuple-element.102) | copy-start | bytes 393220
